TPU v7x, 32 devices: a whole 2x2x4 slice. The times are simulated.
32 devices in a mesh: groups: 2 (over y), expert: 4 (over z), tensor: 4 (over x, core).
Axes of the slice: x: 2, y: 2, z: 4, core: 2. Of those that a mesh axis runs over, the one named last changes fastest.
Arguments:
- source_states: bfloat16 [2048, 2048], P(('groups', 'expert')), parts along dimension 0, may hold values from -6 to 6
- routes: int32 [2048, 2], P(('groups', 'expert')), parts along dimension 0, may hold values from 0 to 3, all different within a row; in each aligned block of 256 rows (0 to 255, 256 to 511, ...) at most 256 rows name the same one
- router_weight: bfloat16 [2048, 4], replicated, may hold values from -0.125 to 0.125
- fc1_weight: bfloat16 [4, 2048, 8192], P('expert', None, 'tensor'), may hold values from -0.125 to 0.125
- fc2_weight: bfloat16 [4, 8192, 2048], P('expert', 'tensor'), may hold values from -0.09375 to 0.09375
- lengths: int32 [8, 8], P(('groups', 'expert')), parts along dimension 0, may hold values from 1 to 48, 256 in all within a row
- lang_ids: int32 [64, 6], P(('groups', 'expert')), parts along dimension 0, may hold values from 0 to 5, each once within a row
- pivot_states: bfloat16 [6, 2048], replicated, may hold values from -480 to 480
- query_weight: bfloat16 [2048, 2048], P(None, 'tensor'), may hold values from -0.125 to 0.125
- key_weight: bfloat16 [2048, 2048], P(None, 'tensor'), may hold values from -0.125 to 0.125
- value_weight: bfloat16 [2048, 2048], P(None, 'tensor'), may hold values from -0.125 to 0.125
- out_weight: bfloat16 [2048, 2048], P('tensor'), may hold values from -0.125 to 0.125
Outputs:
- encoded_states: bfloat16 [2048, 2048], P(('groups', 'expert'), 'tensor'), parts along dimension 0
- decoder_states: bfloat16 [384, 2048], P(('groups', 'expert')), parts along dimension 0
There are 2 independent parts, one for each index of `groups`. A program takes and returns all parts, laid end to end along the dimension named above; an argument that names none is the same for every part. Nothing has to cross between parts.
Inputs may be any that keep to these rules, and one draw needn't show every extreme that they name: `routes`: each token names two different experts; among the 256 tokens of one block no expert is named more than 256 times. `lengths`: each row sums to 256. `lang_ids`: each row names every pivot language once.
All inputs are finite; a program needn't handle non-finite values.
Results may differ from a plain program's by a relative error of at most 0.012.
Values may be sent and summed in bfloat16 or wider, within the bound.
A program may use at most 128 MiB of HBM per device.

v0:
```python
import jax
import jax.numpy as jnp
from jax import lax
from jax.sharding import PartitionSpec as P

HD = 128
EPSILON = 1e-05
NEGATIVE = -1e30


def normalize(values):
    values = values.astype(jnp.float32)
    center = jnp.mean(values, axis=-1, keepdims=True)
    shifted = values - center
    spread = jnp.mean(shifted * shifted, axis=-1, keepdims=True)
    return shifted * lax.rsqrt(spread + EPSILON)


def route_tables(routes, experts, capacity):
    tok_count = routes.shape[0]
    expert_iota = jnp.arange(experts, dtype=jnp.int32)
    chosen = routes[:, :, None] == expert_iota[None, None, :]
    flat_chosen = chosen.reshape(tok_count * 2, experts).astype(jnp.int32)
    before = jnp.cumsum(flat_chosen, axis=0) - flat_chosen
    slots = jnp.sum(before * flat_chosen, axis=1).reshape(tok_count, 2)
    slot_iota = jnp.arange(capacity, dtype=jnp.int32)
    placed = chosen[:, :, :, None] & (slots[:, :, None, None] == slot_iota[None, None, None, :])
    return (chosen, placed.reshape(tok_count, 2, experts * capacity).astype(jnp.bfloat16))


def project_pair(key_weight, value_weight):

    def project(totals, shard_part, offset):
        return (
            jnp.dot(shard_part, key_weight, preferred_element_type=jnp.float32),
            jnp.dot(shard_part, value_weight, preferred_element_type=jnp.float32),
        )

    return project


def shards(
    source_states,
    routes,
    router_weight,
    fc1_weight,
    fc2_weight,
    lengths,
    lang_ids,
    pivot_states,
    query_weight,
    key_weight,
    value_weight,
    out_weight,
):
    tok_count, model_width = source_states.shape
    experts = router_weight.shape[1]
    capacity = 4 * tok_count // experts
    tensor_count = lax.axis_size("tensor")
    column_width = model_width // tensor_count
    column_start = lax.axis_index("tensor") * column_width
    normed = normalize(source_states).astype(jnp.bfloat16)
    logits = jnp.dot(normed, router_weight, preferred_element_type=jnp.float32)
    chosen, placed = route_tables(routes, experts, capacity)
    pair_logits = jnp.sum(jnp.where(chosen, logits[:, None, :], 0.0), axis=2)
    gate_values = jax.nn.sigmoid(pair_logits - pair_logits[:, ::-1])
    occupied = jnp.sum(placed, axis=1)
    outgoing = jnp.einsum("ts,td->sd", occupied, normed, preferred_element_type=jnp.float32)
    outgoing = outgoing.astype(jnp.bfloat16).reshape(experts, capacity, model_width)
    weight_in = fc1_weight[0]
    weight_back = fc2_weight[0]
    arrived = lax.all_to_all(outgoing, "expert", split_axis=0, concat_axis=0, tiled=True)
    row_block = arrived.reshape(-1, model_width)
    hidden = jnp.maximum(
        jnp.dot(row_block, weight_in, preferred_element_type=jnp.float32), 0.0
    ).astype(jnp.bfloat16)
    partial_value = jnp.dot(hidden, weight_back, preferred_element_type=jnp.float32).astype(
        jnp.bfloat16
    )
    partials = partial_value.reshape(arrived.shape)
    zeroed = jnp.zeros((tok_count, key_weight.shape[1]), jnp.float32)
    project = project_pair(key_weight, value_weight)
    own_cols = lax.dynamic_slice_in_dim(source_states, column_start, column_width, 1).astype(
        jnp.float32
    )
    widened = partials.astype(jnp.float32)
    summed = lax.psum_scatter(
        widened.astype(jnp.bfloat16), "tensor", scatter_dimension=2, tiled=True
    )
    returned_rows = lax.all_to_all(summed, "expert", split_axis=0, concat_axis=0, tiled=True)
    picked = jnp.einsum(
        "tks,sd->tkd",
        placed,
        returned_rows.reshape(experts * capacity, column_width),
        preferred_element_type=jnp.float32,
    )
    encoded = (own_cols + jnp.sum(gate_values[:, :, None] * picked, axis=1)).astype(jnp.bfloat16)
    key_sum, value_sum = project(
        (zeroed, zeroed), lax.all_gather(encoded, "tensor", axis=1, tiled=True), jnp.int32(0)
    )
    key_cache = key_sum.astype(jnp.bfloat16)
    value_cache = value_sum.astype(jnp.bfloat16)
    query_count = lengths.shape[1]
    pivot_count = pivot_states.shape[0]
    row_count = query_count * pivot_count
    query_ends = jnp.cumsum(lengths[0])
    positions = jnp.arange(tok_count, dtype=jnp.int32)
    key_owner = jnp.sum((positions[:, None] >= query_ends[None, :]).astype(jnp.int32), axis=1)
    row_owner = jnp.arange(row_count, dtype=jnp.int32) // pivot_count
    allowed = row_owner[:, None] == key_owner[None, :]
    language_pick = (
        lang_ids.reshape(-1)[:, None] == jnp.arange(pivot_count, dtype=jnp.int32)[None, :]
    ).astype(jnp.bfloat16)
    decoder_in = jnp.dot(language_pick, pivot_states, preferred_element_type=jnp.float32).astype(
        jnp.bfloat16
    )
    queries = jnp.dot(decoder_in, query_weight, preferred_element_type=jnp.float32).astype(
        jnp.bfloat16
    )
    head_local = queries.shape[1] // HD
    query_heads = queries.reshape(row_count, head_local, HD)
    key_heads = key_cache.reshape(tok_count, head_local, HD)
    value_heads = value_cache.reshape(tok_count, head_local, HD)
    scores = jnp.einsum(
        "rhe,the->hrt", query_heads, key_heads, preferred_element_type=jnp.float32
    ) * HD ** (-0.5)
    scores = jnp.where(allowed[None], scores, NEGATIVE)
    row_max = jnp.max(scores, axis=2, keepdims=True)
    weights = jnp.exp(scores - row_max)
    attention = (weights / jnp.sum(weights, axis=2, keepdims=True)).astype(jnp.bfloat16)
    context = jnp.einsum(
        "hrt,the->rhe", attention, value_heads, preferred_element_type=jnp.float32
    ).astype(jnp.bfloat16)
    partial_out = jnp.dot(
        context.reshape(row_count, head_local * HD), out_weight, preferred_element_type=jnp.float32
    )
    attn_total = lax.psum(partial_out.astype(jnp.bfloat16), "tensor").astype(jnp.float32)
    decoded = normalize(decoder_in.astype(jnp.float32) + attn_total).astype(jnp.bfloat16)
    return (encoded, decoded)


def solution(mesh):
    in_specs = (
        P(("groups", "expert"), None),
        P(("groups", "expert"), None),
        P(),
        P("expert", None, "tensor"),
        P("expert", "tensor", None),
        P(("groups", "expert"), None),
        P(("groups", "expert"), None),
        P(),
        P(None, "tensor"),
        P(None, "tensor"),
        P(None, "tensor"),
        P("tensor", None),
    )
    out_specs = (P(("groups", "expert"), "tensor"), P(("groups", "expert"), None))
    return jax.shard_map(shards, mesh=mesh, in_specs=in_specs, out_specs=out_specs, check_vma=False)
```

profile of v0, /device:TPU:0, one launch (start us, length us, event | category | flops | bytes accessed | tf_op | source)
XLA Modules:
  0.0 283.3 jit_solution(7772362713964266053)
XLA Ops:
  7.2 1.0 copy.39
  8.5 0.7 iota_compare_fusion.6
  9.2 1.2 reduce-window.18
  10.4 0.2 slice_reduce_fusion
  11.3 1.3 fusion.32
  12.7 2.1 copy.42
  14.7 0.2 convert_reduce_fusion
  15.0 0.4 fusion.14
  15.4 0.4 copy-done.2
  15.8 1.4 convolution_convert_fusion
  17.2 99.4 %all_to_all.10 = bf16[4,256,2048]{2,1,0:T(8,128)(2,1)} all-to-all(bf16[4,256,2048]{2,1,0:T(8,128)(2,1)S(1)} %bitcast.88), channel_id=1, replica_groups=mesh['groups'=2,'expert'=4,'tensor'=4] {'expert'}, dimensions={0} | all-to-all | bytes 8388608 | tf_op jit(solution)/shard_map/all_to_all | solution.py:72
  116.5 25.4 %fusion.7 = bf16[1024,2048]{1,0:T(8,128)(2,1)} fusion(bf16[1,2048,2048]{2,1,0:T(8,128)(2,1)} %param.16, bf16[1024,2048]{1,0:T(8,128)(2,1)} %bitcast.90, bf16[1,2048,2048]{2,1,0:T(8,128)(2,1)} %param.15), kind=kOutput, calls=%fused_computation.6 | convolution fusion | flops 17186160640 | bytes 25165824 | tf_op jit(solution)/shard_map/dot_general | solution.py:77
  142.0 44.0 %reduce-scatter.2.cloned.1.call-done = bf16[4,256,512]{2,1,0:T(8,128)(2,1)} async-done(((bf16[4,256,2048]{2,1,0:T(8,128)(2,1)}), bf16[4,256,512]{2,1,0:T(8,128)(2,1)}) %reduce-scatter.2.cloned.1.call-update) | async-done | bytes 1048592 | tf_op jit(solution)/shard_map/reduce_scatter | solution.py:87
  186.0 4.6 %all-to-all-start.1 = ((bf16[4,256,512]{2,1,0:T(8,128)(2,1)}), bf16[4,256,512]{2,1,0:T(8,128)(2,1)}, u32[]{:S(2)}, u32[]{:S(2)}) async-start(bf16[4,256,512]{2,1,0:T(8,128)(2,1)} %reduce-scatter.2.cloned.1.call-done), calls=%async_computation.2 | async-start | bytes 2097152 | tf_op jit(solution)/shard_map/all_to_all | solution.py:90
  190.6 0.4 fusion.54
  191.2 25.2 %all-to-all-done.1 = bf16[4,256,512]{2,1,0:T(8,128)(2,1)} async-done(((bf16[4,256,512]{2,1,0:T(8,128)(2,1)}), bf16[4,256,512]{2,1,0:T(8,128)(2,1)}, u32[]{:S(2)}, u32[]{:S(2)}) %all-to-all-start.1) | async-done | bytes 1048608 | tf_op jit(solution)/shard_map/all_to_all | solution.py:90
  216.4 2.3 fusion.22
  218.7 0.8 add_convert_fusion
  219.6 0.2 reduce-window.20
  220.0 0.2 convolution_convert_fusion.2
  220.3 2.1 fusion.31
  222.3 12.2 %all-gather.2.cloned.1.call-done = bf16[256,2048]{1,0:T(8,128)(2,1)} async-done(((bf16[256,512]{1,0:T(8,128)(2,1)}), bf16[256,2048]{1,0:T(8,128)(2,1)}) %all-gather.2.cloned.1.call-update) | async-done | bytes 1048592 | tf_op jit(solution)/shard_map/all_gather | solution.py:99
  234.5 2.1 fusion.27
  236.6 0.2 fusion.28
  236.8 0.2 fusion.56
  237.0 0.7 fusion.26
  237.8 0.4 fusion.30
  238.1 2.8 convolution_convert_fusion.1
  240.9 31.8 %all-reduce.2.cloned.1.call-done = bf16[48,2048]{1,0:T(8,128)(2,1)} async-done(((bf16[48,2048]{1,0:T(8,128)(2,1)}), bf16[48,2048]{1,0:T(8,128)(2,1)}) %all-reduce.2.cloned.1.call-update) | async-done | bytes 196624 | tf_op jit(solution)/shard_map/psum | solution.py:137
  272.8 1.1 fusion.37
  273.8 1.1 multiply_reduce_fusion
  275.0 1.7 multiply_convert_fusion
  (45 shorter events, 1.5 us)
Async XLA Ops:
  7.2 227.4 %copy-start = (bf16[2048,512]{1,0:T(8,128)(2,1)S(1)}, bf16[2048,512]{1,0:T(8,128)(2,1)}, u32[]{:S(2)}) copy-start(bf16[2048,512]{1,0:T(8,128)(2,1)} %param.21) | copy-start | bytes 6291460
  7.2 7.6 %copy-start.1 = (bf16[256,2048]{1,0:T(8,128)(2,1)S(1)}, bf16[256,2048]{1,0:T(8,128)(2,1)}, u32[]{:S(2)}) copy-start(bf16[256,2048]{1,0:T(8,128)(2,1)} %param.12) | copy-start | bytes 3145732
  7.2 178.8 %reduce-scatter.2.cloned.1.call-start = ((), (), s32[]{:S(2)}) async-start(), calls=%async_computation.3 | async-start | bytes 5242880 | tf_op jit(solution)/shard_map/reduce_scatter | solution.py:87
  14.7 1.0 copy-start.2
  141.9 48.6 %copy-start.8 = (bf16[2048,4]{0,1:T(4,128)(2,1)S(1)}, bf16[2048,4]{0,1:T(4,128)(2,1)}, u32[]{:S(2)}) copy-start(bf16[2048,4]{0,1:T(4,128)(2,1)} %param.14) | copy-start | bytes 49156
  141.9 49.1 %copy-start.4 = (s32[256,2]{0,1:T(2,128)S(1)}, s32[256,2]{0,1:T(2,128)}, u32[]{:S(2)}) copy-start(s32[256,2]{0,1:T(2,128)} %param.13) | copy-start | bytes 6148
  186.0 30.4 %all-to-all-start.1 = ((bf16[4,256,512]{2,1,0:T(8,128)(2,1)}), bf16[4,256,512]{2,1,0:T(8,128)(2,1)}, u32[]{:S(2)}, u32[]{:S(2)}) async-start(bf16[4,256,512]{2,1,0:T(8,128)(2,1)} %reduce-scatter.2.cloned.1.call-done), calls=%async_computation.2 | async-start | bytes 2097152 | tf_op jit(solution)/shard_map/all_to_all | solution.py:90
  190.6 44.0 %all-gather.2.cloned.1.call-start = ((), (), s32[]{:S(2)}) async-start(), calls=%async_computation.4 | async-start | bytes 1310720 | tf_op jit(solution)/shard_map/all_gather | solution.py:99
  191.2 28.4 %copy-start.5 = (s32[8,6]{1,0:T(8,128)S(1)}, s32[8,6]{1,0:T(8,128)}, u32[]{:S(2)}) copy-start(s32[8,6]{1,0:T(8,128)} %param.18) | copy-start | bytes 580
  191.2 28.5 %copy-start.9 = (s32[1,8]{1,0:T(1,128)S(1)}, s32[1,8]{1,0:T(1,128)}, u32[]{:S(2)}) copy-start(s32[1,8]{1,0:T(1,128)} %param.17) | copy-start | bytes 100
  191.2 28.8 %copy-start.3 = (bf16[6,2048]{1,0:T(8,128)(2,1)S(1)}, bf16[6,2048]{1,0:T(8,128)(2,1)}, u32[]{:S(2)}) copy-start(bf16[6,2048]{1,0:T(8,128)(2,1)} %param.19) | copy-start | bytes 73732
  219.5 53.3 %all-reduce.2.cloned.1.call-start = ((), (), s32[]{:S(2)}) async-start(), calls=%async_computation.5 | async-start | bytes 393216 | tf_op jit(solution)/shard_map/psum | solution.py:137
  234.5 2.5 copy-start.6
  234.5 2.5 copy-start.7
Sparse Core Ops, SparseCore 0:
  142.0 43.8 reduce-scatter.1
  219.6 14.8 all-gather.1
  241.0 31.6 all-reduce.1
where the time goes:
time: 284 us; the launch traced here: 283 us
  waiting for transfers between devices  113 us (40%)
  blocking collectives  99.4 us (35%)
  matrix products  37.9 us (13%)
  between operations  14 us (5%)
  other arithmetic  9.69 us (3%)
  starting transfers between devices  4.68 us (2%)
  local copies, waits for them, and re-layouts  4.36 us (2%)
    all_to_all x1, blocking collectives, shards(): lax.all_to_all(outgoing, 'expert', split_axis=0, concat_axis=0, tiled=True)  99.4 us
    reduce_scatter x1, waiting for transfers between devices, shards(): lax.psum_scatter(widened.astype(jnp.bfloat16), 'tensor', scatter_dimensio...  44 us
    psum x1, waiting for transfers between devices, shards(): lax.psum(partial_out.astype(jnp.bfloat16), 'tensor').astype(jnp.float32)  31.8 us
    dot_general x1, matrix products, shards(): jnp.dot(hidden, weight_back, preferred_element_type=jnp.float32)  25.4 us
    all_to_all x1, waiting for transfers between devices, shards(): lax.all_to_all(summed, 'expert', split_axis=0, concat_axis=0, tiled=True)  25.2 us
    all_gather x1, waiting for transfers between devices, shards(): lax.all_gather(encoded, 'tensor', axis=1, tiled=True)  12.2 us
  transfers between devices with their start and end apart: 4, of which 4 were waited for; matrix products, arithmetic and copies ran while one was open for 1% of the time, Pallas kernels for 0%

commit v1 on v0

--- a/solution.py
+++ b/solution.py
@@ -53,6 +53,10 @@
     value_weight,
     out_weight,
 ):
+
+    def fill_members_all_all(target):
+        return lax.all_gather(target, axis_name="tensor").sum(axis=0)
+
     tok_count, model_width = source_states.shape
     experts = router_weight.shape[1]
     capacity = 4 * tok_count // experts
@@ -134,7 +138,7 @@
     partial_out = jnp.dot(
         context.reshape(row_count, head_local * HD), out_weight, preferred_element_type=jnp.float32
     )
-    attn_total = lax.psum(partial_out.astype(jnp.bfloat16), "tensor").astype(jnp.float32)
+    attn_total = fill_members_all_all(partial_out.astype(jnp.bfloat16)).astype(jnp.float32)
     decoded = normalize(decoder_in.astype(jnp.float32) + attn_total).astype(jnp.bfloat16)
     return (encoded, decoded)
 

time: 284 us -> 259 us (0.912)
  waiting for transfers between devices: 113 us -> 81.5 us
  blocking collectives: 99.4 us -> 108 us
    psum x1 -> x0, waiting for transfers between devices: 31.8 us -> none  [shards(): lax.psum(partial_out.astype(jnp.bfloat16), 'tensor').astype(jnp.float32)]
    all_gather x0 -> x1, blocking collectives: none -> 9.05 us  [fill_members_all_all(): return lax.all_gather(target, axis_name='tensor').sum(axis=0)]
  transfers between devices with their start and end apart: 4 -> 3, of which waited for: 4 -> 3; matrix products, arithmetic and copies ran while one was open for 1% -> 1% of each run, Pallas kernels for 0% -> 0%
where the time goes in v1:
time: 259 us
  blocking collectives  108 us (42%)
  waiting for transfers between devices  81.5 us (31%)
  matrix products  37.2 us (14%)
  between operations  14.3 us (6%)
  other arithmetic  8.18 us (3%)
  starting transfers between devices  4.64 us (2%)
  local copies, waits for them, and re-layouts  4.36 us (2%)
    all_to_all x1, blocking collectives, shards(): lax.all_to_all(outgoing, 'expert', split_axis=0, concat_axis=0, tiled=True)  99.4 us
    reduce_scatter x1, waiting for transfers between devices, shards(): lax.psum_scatter(widened.astype(jnp.bfloat16), 'tensor', scatter_dimensio...  44 us
    dot_general x1, matrix products, shards(): jnp.dot(hidden, weight_back, preferred_element_type=jnp.float32)  25.4 us
    all_to_all x1, waiting for transfers between devices, shards(): lax.all_to_all(summed, 'expert', split_axis=0, concat_axis=0, tiled=True)  25.2 us
    all_gather x1, waiting for transfers between devices, shards(): lax.all_gather(encoded, 'tensor', axis=1, tiled=True)  12.2 us
    all_gather x1, blocking collectives, fill_members_all_all(): return lax.all_gather(target, axis_name='tensor').sum(axis=0)  9.05 us
  transfers between devices with their start and end apart: 3, of which 3 were waited for; matrix products, arithmetic and copies ran while one was open for 1% of the time, Pallas kernels for 0%

profile of v1, /device:TPU:0, one launch (start us, length us, event | category | flops | bytes accessed | tf_op | source)
XLA Modules:
  0.0 258.5 jit_solution(7010802427442146056)
XLA Ops:
  7.2 1.0 copy.39
  8.5 0.7 iota_compare_fusion.6
  9.2 1.2 reduce-window.18
  10.4 0.2 slice_reduce_fusion
  11.3 1.3 fusion.32
  12.7 2.1 copy.42
  14.7 0.2 convert_reduce_fusion
  15.0 0.4 fusion.14
  15.4 0.4 copy-done.2
  15.8 1.4 convolution_convert_fusion
  17.2 99.4 %all_to_all.10 = bf16[4,256,2048]{2,1,0:T(8,128)(2,1)} all-to-all(bf16[4,256,2048]{2,1,0:T(8,128)(2,1)S(1)} %bitcast.89), channel_id=1, replica_groups=mesh['groups'=2,'expert'=4,'tensor'=4] {'expert'}, dimensions={0} | all-to-all | bytes 8388608 | tf_op jit(solution)/shard_map/all_to_all | solution.py:76
  116.6 25.4 %fusion.7 = bf16[1024,2048]{1,0:T(8,128)(2,1)} fusion(bf16[1,2048,2048]{2,1,0:T(8,128)(2,1)} %param.16, bf16[1024,2048]{1,0:T(8,128)(2,1)} %bitcast.91, bf16[1,2048,2048]{2,1,0:T(8,128)(2,1)} %param.15), kind=kOutput, calls=%fused_computation.6 | convolution fusion | flops 17186160640 | bytes 25165824 | tf_op jit(solution)/shard_map/dot_general | solution.py:81
  142.0 44.0 %reduce-scatter.2.cloned.1.call-done = bf16[4,256,512]{2,1,0:T(8,128)(2,1)} async-done(((bf16[4,256,2048]{2,1,0:T(8,128)(2,1)}), bf16[4,256,512]{2,1,0:T(8,128)(2,1)}) %reduce-scatter.2.cloned.1.call-update) | async-done | bytes 1048592 | tf_op jit(solution)/shard_map/reduce_scatter | solution.py:91
  186.0 4.6 %all-to-all-start.1 = ((bf16[4,256,512]{2,1,0:T(8,128)(2,1)}), bf16[4,256,512]{2,1,0:T(8,128)(2,1)}, u32[]{:S(2)}, u32[]{:S(2)}) async-start(bf16[4,256,512]{2,1,0:T(8,128)(2,1)} %reduce-scatter.2.cloned.1.call-done), calls=%async_computation.2 | async-start | bytes 2097152 | tf_op jit(solution)/shard_map/all_to_all | solution.py:94
  190.6 0.4 fusion.54
  191.2 25.2 %all-to-all-done.1 = bf16[4,256,512]{2,1,0:T(8,128)(2,1)} async-done(((bf16[4,256,512]{2,1,0:T(8,128)(2,1)}), bf16[4,256,512]{2,1,0:T(8,128)(2,1)}, u32[]{:S(2)}, u32[]{:S(2)}) %all-to-all-start.1) | async-done | bytes 1048608 | tf_op jit(solution)/shard_map/all_to_all | solution.py:94
  216.4 2.3 fusion.22
  218.7 0.8 add_convert_fusion
  219.6 0.2 reduce-window.20
  220.0 0.2 convolution_convert_fusion.2
  220.2 2.1 fusion.31
  222.3 12.2 %all-gather.3.cloned.1.call-done = bf16[256,2048]{1,0:T(8,128)(2,1)} async-done(((bf16[256,512]{1,0:T(8,128)(2,1)}), bf16[256,2048]{1,0:T(8,128)(2,1)}) %all-gather.3.cloned.1.call-update) | async-done | bytes 1048592 | tf_op jit(solution)/shard_map/all_gather | solution.py:103
  234.5 2.1 fusion.27
  236.6 0.2 fusion.28
  236.8 0.2 fusion.56
  237.0 0.7 fusion.26
  237.7 0.4 fusion.30
  238.1 2.1 convolution_convert_fusion.1
  240.2 9.1 %all-gather = bf16[192,2048]{1,0:T(8,128)(2,1)} all-gather(bf16[48,2048]{1,0:T(8,128)(2,1)S(1)} %convolution_convert_fusion.1), channel_id=2, replica_groups=mesh['groups'=2,'expert'=4,'tensor'=4] {'tensor'}, dimensions={0}, use_global_device_ids=true | all-gather | bytes 983040 | tf_op jit(solution)/shard_map/all_gather | solution.py:58
  249.2 1.3 reduce_sum.116
  250.7 0.2 multiply_reduce_fusion
  250.9 0.8 multiply_convert_fusion
  (44 shorter events, 1.6 us)
Async XLA Ops:
  7.2 227.3 %copy-start = (bf16[2048,512]{1,0:T(8,128)(2,1)S(1)}, bf16[2048,512]{1,0:T(8,128)(2,1)}, u32[]{:S(2)}) copy-start(bf16[2048,512]{1,0:T(8,128)(2,1)} %param.21) | copy-start | bytes 6291460
  7.2 7.6 %copy-start.1 = (bf16[256,2048]{1,0:T(8,128)(2,1)S(1)}, bf16[256,2048]{1,0:T(8,128)(2,1)}, u32[]{:S(2)}) copy-start(bf16[256,2048]{1,0:T(8,128)(2,1)} %param.12) | copy-start | bytes 3145732
  7.2 178.8 %reduce-scatter.2.cloned.1.call-start = ((), (), s32[]{:S(2)}) async-start(), calls=%async_computation.3 | async-start | bytes 5242880 | tf_op jit(solution)/shard_map/reduce_scatter | solution.py:91
  14.7 1.0 copy-start.2
  141.9 48.7 %copy-start.8 = (bf16[2048,4]{0,1:T(4,128)(2,1)S(1)}, bf16[2048,4]{0,1:T(4,128)(2,1)}, u32[]{:S(2)}) copy-start(bf16[2048,4]{0,1:T(4,128)(2,1)} %param.14) | copy-start | bytes 49156
  141.9 49.1 %copy-start.4 = (s32[256,2]{0,1:T(2,128)S(1)}, s32[256,2]{0,1:T(2,128)}, u32[]{:S(2)}) copy-start(s32[256,2]{0,1:T(2,128)} %param.13) | copy-start | bytes 6148
  186.0 30.4 %all-to-all-start.1 = ((bf16[4,256,512]{2,1,0:T(8,128)(2,1)}), bf16[4,256,512]{2,1,0:T(8,128)(2,1)}, u32[]{:S(2)}, u32[]{:S(2)}) async-start(bf16[4,256,512]{2,1,0:T(8,128)(2,1)} %reduce-scatter.2.cloned.1.call-done), calls=%async_computation.2 | async-start | bytes 2097152 | tf_op jit(solution)/shard_map/all_to_all | solution.py:94
  190.6 43.9 %all-gather.3.cloned.1.call-start = ((), (), s32[]{:S(2)}) async-start(), calls=%async_computation.4 | async-start | bytes 1310720 | tf_op jit(solution)/shard_map/all_gather | solution.py:103
  191.2 28.3 %copy-start.5 = (s32[8,6]{1,0:T(8,128)S(1)}, s32[8,6]{1,0:T(8,128)}, u32[]{:S(2)}) copy-start(s32[8,6]{1,0:T(8,128)} %param.18) | copy-start | bytes 580
  191.2 28.4 %copy-start.9 = (s32[1,8]{1,0:T(1,128)S(1)}, s32[1,8]{1,0:T(1,128)}, u32[]{:S(2)}) copy-start(s32[1,8]{1,0:T(1,128)} %param.17) | copy-start | bytes 100
  191.2 28.8 %copy-start.3 = (bf16[6,2048]{1,0:T(8,128)(2,1)S(1)}, bf16[6,2048]{1,0:T(8,128)(2,1)}, u32[]{:S(2)}) copy-start(bf16[6,2048]{1,0:T(8,128)(2,1)} %param.19) | copy-start | bytes 73732
  234.5 2.5 copy-start.6
  234.5 2.5 copy-start.7
Sparse Core Ops, SparseCore 0:
  142.1 43.8 reduce-scatter.1
  219.6 14.8 all-gather.2
